TPU v7x, 32 devices: a whole 2x2x4 slice. The times are simulated.
32 devices in a mesh: seq: 4 (over x, core), view: 4 (over z), dp: 2 (over y).
Axes of the slice: x: 2, y: 2, z: 4, core: 2. Of those that a mesh axis runs over, the one named last changes fastest.
Arguments:
- latent: bfloat16 [8, 8, 64, 1152], P(('dp', 'view'), 'seq'), parts along dimension 0, may hold values from -6 to 6
- condition: bfloat16 [8, 8, 64, 1152], P(('dp', 'view'), 'seq'), parts along dimension 0, may hold values from -6 to 6
- cycle_order: int32 [8], P('dp'), parts along dimension 0, may hold values from 0 to 3, each once
- live_frames: int32 [8], P('dp'), parts along dimension 0, may hold values from 4 to 8
- w_qkv_ctrl: bfloat16 [1152, 3456], P('seq'), may hold values from -0.1875 to 0.1875
- w_out_ctrl: bfloat16 [1152, 1152], P('seq'), may hold values from -0.1875 to 0.1875
- w_join: bfloat16 [1152, 1152], P('seq'), may hold values from -0.1875 to 0.1875
- w_qkv_space: bfloat16 [1152, 3456], P('seq'), may hold values from -0.1875 to 0.1875
- w_out_space: bfloat16 [1152, 1152], P('seq'), may hold values from -0.1875 to 0.1875
- w_qkv_time: bfloat16 [1152, 3456], P('seq'), may hold values from -0.1875 to 0.1875
- w_out_time: bfloat16 [1152, 1152], P('seq'), may hold values from -0.1875 to 0.1875
- mod_ctrl: float32 [6, 1152], P('dp'), parts along dimension 0, may hold values from -3 to 3
- mod_space: float32 [6, 1152], P('dp'), parts along dimension 0, may hold values from -3 to 3
- mod_time: float32 [6, 1152], P('dp'), parts along dimension 0, may hold values from -3 to 3
- qk_gain: float32 [3, 2, 72], replicated, may hold values from 0.5 to 3.5, as said below
Outputs:
- result: bfloat16 [8, 8, 64, 1152], P(('dp', 'view'), None, 'seq'), parts along dimension 0
There are 2 independent parts, one for each index of `dp`. A program takes and returns all parts, laid end to end along the dimension named above; an argument that names none is the same for every part. Nothing has to cross between parts.
Inputs may be any that keep to these rules, and one draw needn't show every extreme that they name: `cycle_order`: a permutation of the 4 cameras. `qk_gain`: positive gains.
All inputs are finite; a program needn't handle non-finite values.
Results may differ from a plain program's by a relative error of at most 0.01.
Values may be sent and summed in bfloat16 or wider, within the bound.
A program may use at most 192 MiB of HBM per device.

v0:
```python
import jax
import jax.numpy as jnp
from jax import lax
from jax.experimental import pallas as pl
from jax.experimental.pallas import tpu as pltpu
from jax.sharding import PartitionSpec as P

HEADS = 16

epsilon = 1e-06
masked_score = -1e30


def layer_norm(stream):
    average = jnp.mean(stream, -1, keepdims=True)
    centred = stream - average
    spread = jnp.mean(centred * centred, -1, keepdims=True)
    return centred * lax.rsqrt(spread + epsilon)


def modulate(stream, modulation):
    return (layer_norm(stream) * (1.0 + modulation[1]) + modulation[0]).astype(jnp.bfloat16)


def unit_rms(tensor):
    return tensor * lax.rsqrt(jnp.mean(tensor * tensor, -1, keepdims=True) + epsilon)


def collect_rows(weight, dp_size):
    rows, columns = weight.shape
    shares = weight.reshape(dp_size, rows // dp_size, columns)
    own_share = lax.dynamic_index_in_dim(shares, lax.axis_index("dp"), 0, keepdims=False)
    return lax.all_gather(own_share, ("seq", "dp"), axis=0, tiled=True)


def tile_of(size, unit, largest):
    tiles = [t for t in range(unit, min(size, largest) + 1, unit) if size % t == 0]
    return tiles[-1] if tiles else size


def matmul_kernel(x_ref, w_ref, out_ref):
    out_ref[...] = jnp.dot(x_ref[...], w_ref[...], preferred_element_type=jnp.float32)


def project(inputs, weight):
    rows, depth = inputs.shape
    columns = weight.shape[1]
    row_tile = tile_of(rows, 16, 1024)
    column_tile = tile_of(columns, 128, 512)
    return pl.pallas_call(
        matmul_kernel,
        grid=(rows // row_tile, columns // column_tile),
        in_specs=[
            pl.BlockSpec((row_tile, depth), lambda i, j: (i, 0)),
            pl.BlockSpec((depth, column_tile), lambda i, j: (0, j)),
        ],
        out_specs=pl.BlockSpec((row_tile, column_tile), lambda i, j: (i, j)),
        out_shape=jax.ShapeDtypeStruct((rows, columns), jnp.float32),
        compiler_params=pltpu.CompilerParams(vmem_limit_bytes=24 * 2**20),
        cost_estimate=pl.CostEstimate(
            flops=2 * rows * depth * columns,
            bytes_accessed=2 * (rows + columns) * depth + 4 * rows * columns,
            transcendentals=0,
        ),
    )(inputs, weight)


def heads_of(packed, gain_pair, head_count):
    tokens = packed.shape[0]
    pieces = packed.reshape(tokens, 3, head_count, -1).transpose(1, 2, 0, 3)
    head_size = pieces.shape[-1]
    queries = unit_rms(pieces[0]) * gain_pair[0] * head_size ** (-0.5)
    keys = unit_rms(pieces[1]) * gain_pair[1]
    return queries.astype(jnp.bfloat16), keys.astype(jnp.bfloat16), pieces[2].astype(jnp.bfloat16)


def attend(queries, keys, values, allowed):
    scores = jnp.einsum("bqd,bkd->bqk", queries, keys, preferred_element_type=jnp.float32)
    if allowed is not None:
        scores = jnp.where(allowed[None], scores, masked_score)
    terms = jnp.exp(scores - jnp.max(scores, -1, keepdims=True))
    totals = jnp.sum(terms, -1, keepdims=True)
    mixed = jnp.einsum("bqk,bkd->bqd", terms.astype(jnp.bfloat16), values, preferred_element_type=jnp.float32)
    return (mixed / totals).astype(jnp.bfloat16)


def camera_mask(cycle_order):
    cameras = cycle_order.shape[0]
    onehot = (cycle_order[:, None] == jnp.arange(cameras, dtype=jnp.int32)[None, :]).astype(jnp.float32)
    after = jnp.roll(onehot, -1, axis=0)
    follow = jnp.dot(onehot.T, after)
    return follow + follow.T + jnp.eye(cameras, dtype=jnp.float32) > 0.5


def per_device(
    view_size,
    dp_size,
    latent,
    condition,
    cycle_order,
    live_frames,
    w_qkv_ctrl,
    w_out_ctrl,
    w_join,
    w_qkv_space,
    w_out_space,
    w_qkv_time,
    w_out_time,
    mod_ctrl,
    mod_space,
    mod_time,
    qk_gain,
):
    frames_here, patches, width = latent.shape[1:]
    tokens = frames_here * patches
    head_size = width // HEADS
    view = lax.axis_index("view")
    view_heads = HEADS // view_size
    collect = lambda weight: collect_rows(weight, dp_size)

    qkv_ctrl = collect(w_qkv_ctrl)
    out_ctrl = collect(w_out_ctrl)
    join = collect(w_join)
    columns = w_qkv_space.reshape(-1, 3, view_size, width // view_size)
    columns = lax.dynamic_index_in_dim(columns, view, 2, keepdims=False)
    qkv_space = collect(columns.reshape(-1, 3 * width // view_size))
    out_space = collect(w_out_space)
    qkv_time = collect(w_qkv_time)
    out_time = collect(w_out_time)

    base = latent.reshape(tokens, width).astype(jnp.float32)
    ctrl_in = base + condition.reshape(tokens, width).astype(jnp.float32)
    packed = project(modulate(ctrl_in, mod_ctrl), qkv_ctrl)
    parts = heads_of(packed, qk_gain[0], HEADS)
    by_frame = [part.reshape(HEADS * frames_here, patches, head_size) for part in parts]
    attended = attend(*by_frame, None).reshape(HEADS, tokens, head_size)
    flat = attended.transpose(1, 0, 2).reshape(tokens, width)
    control = (ctrl_in + mod_ctrl[2] * project(flat, out_ctrl)).astype(jnp.bfloat16)
    joined = base + project(control, join)

    normed = modulate(joined, mod_space)
    upward, downward = [normed], [normed]
    for _ in range(view_size - 1):
        upward.append(lax.ppermute(upward[-1], "view", [(i, i + 1) for i in range(view_size - 1)]))
        downward.append(lax.ppermute(downward[-1], "view", [(i + 1, i) for i in range(view_size - 1)]))
    everyone = [normed] + [jnp.where(view >= t, upward[t], downward[view_size - t]) for t in range(1, view_size)]
    cameras = (view - jnp.arange(view_size)) % view_size
    everyone = jnp.stack(everyone).reshape(view_size * tokens, width)
    packed = project(everyone, qkv_space)
    parts = heads_of(packed, qk_gain[1], view_heads)
    by_frame = [
        part.reshape(view_heads, view_size, frames_here, patches, head_size)
        .transpose(0, 2, 1, 3, 4)
        .reshape(view_heads * frames_here, view_size * patches, head_size)
        for part in parts
    ]
    near = camera_mask(cycle_order)[cameras][:, cameras]
    near = jnp.repeat(jnp.repeat(near, patches, 0), patches, 1)
    attended = attend(*by_frame, near).reshape(view_heads, frames_here, view_size, patches, head_size)
    attended = attended.transpose(2, 1, 3, 0, 4).reshape(view_size, tokens, width // view_size)
    attended = lax.all_to_all(attended[cameras], "view", split_axis=0, concat_axis=0, tiled=True)
    flat = attended.transpose(1, 0, 2).reshape(tokens, width)
    spaced = (joined + mod_space[2] * project(flat, out_space)).astype(jnp.bfloat16)

    spaced = spaced.reshape(1, frames_here, patches, width)
    patched = lax.all_to_all(spaced, "seq", split_axis=2, concat_axis=1, tiled=True)
    frames, patch_here = patched.shape[1:3]
    stream = patched.reshape(frames * patch_here, width).astype(jnp.float32)
    packed = project(modulate(stream, mod_time), qkv_time)
    parts = heads_of(packed, qk_gain[2], HEADS)
    own_live = lax.dynamic_index_in_dim(live_frames, view, 0, keepdims=False)
    place = jnp.arange(frames * patch_here, dtype=jnp.int32)
    same = place[:, None] % patch_here == place[None, :] % patch_here
    alive = place[None, :] // patch_here < own_live
    attended = attend(*parts, same & alive)
    flat = attended.transpose(1, 0, 2).reshape(frames * patch_here, width)
    result = stream + mod_time[2] * project(flat, out_time)
    return result.astype(jnp.bfloat16).reshape(patched.shape)


def solution(mesh):
    placed = (
        P(("dp", "view"), "seq", None, None),
        P(("dp", "view"), "seq", None, None),
        P("dp"),
        P("dp"),
        P("seq", None),
        P("seq", None),
        P("seq", None),
        P("seq", None),
        P("seq", None),
        P("seq", None),
        P("seq", None),
        P("dp", None),
        P("dp", None),
        P("dp", None),
        P(),
    )
    sizes = mesh.shape["view"], mesh.shape["dp"]

    def run(*arrays):
        return per_device(*sizes, *arrays)

    return jax.shard_map(
        run,
        mesh=mesh,
        in_specs=placed,
        out_specs=P(("dp", "view"), None, "seq", None),
        check_vma=False,
    )
```

profile of v0, /device:TPU:0, one launch (start us, length us, event | category | flops | bytes accessed | tf_op | source)
XLA Modules:
  0.0 290.2 jit_solution(397183115427384940)
XLA Ops:
  11.0 3.5 %reshape.451 = bf16[288,3,4,288]{3,2,1,0:T(4,128)(2,1)S(1)} reshape(bf16[288,3456]{1,0:T(8,128)(2,1)} %param.22) | data formatting | bytes 3981312 | tf_op jit(solution)/shard_map/reshape | solution.py:124
  14.4 4.6 %dynamic-slice_reduce_fusion = bf16[288,3,288]{2,1,0:T(4,128)(2,1)S(1)} fusion(bf16[288,3,4,288]{3,2,1,0:T(4,128)(2,1)S(1)} %reshape.451, s32[]{:T(128)S(6)} %select_n.111), kind=kLoop, calls=%fused_computation.12 | loop fusion | bytes 995332 | tf_op jit(solution)/shard_map/jit(dynamic_index_in_dim)/dynamic_slice | solution.py:125
  21.3 2.4 constant_dynamic-slice_fusion.1
  26.2 38.4 %all-gather.15.cloned.1.call-done = bf16[1,1152,3456]{2,1,0:T(8,128)(2,1)} async-done(((bf16[1,144,3456]{2,1,0:T(8,128)(2,1)}), bf16[1,1152,3456]{2,1,0:T(8,128)(2,1)}) %all-gather.15.cloned.1.call-update) | async-done | bytes 7962640 | tf_op jit(solution)/shard_map/all_gather | solution.py:33
  64.7 3.3 %copy-done.3 = bf16[1,1152,3456]{2,1,0:T(8,128)(2,1)S(1)} copy-done((bf16[1,1152,3456]{2,1,0:T(8,128)(2,1)S(1)}, bf16[1,1152,3456]{2,1,0:T(8,128)(2,1)}, u32[]{:S(2)}) %copy-start.3) | copy-done | bytes 7962648
  67.9 3.9 %shard_map.145 = f32[128,3456]{1,0:T(8,128)S(1)} custom-call(bf16[128,1152]{1,0:T(8,128)(2,1)S(1)} %add_convert_fusion.3.x_ref, bf16[1152,3456]{1,0:T(8,128)(2,1)S(1)} %bitcast.181), custom_call_target="tpu_custom_call" | custom-call | flops 1019215872 | bytes 10027008 | tf_op jit(solution)/shard_map/pallas_call | solution.py:50
  71.8 1.8 copy.77
  81.4 15.4 %all-gather.17.cloned.1.call-done = bf16[1,1152,1152]{2,1,0:T(8,128)(2,1)} async-done(((bf16[1,144,1152]{2,1,0:T(8,128)(2,1)}), bf16[1,1152,1152]{2,1,0:T(8,128)(2,1)}) %all-gather.17.cloned.1.call-update) | async-done | bytes 2654224 | tf_op jit(solution)/shard_map/all_gather | solution.py:33
  96.8 1.7 copy-done.7
  100.0 29.0 %all-gather.19.cloned.1.call-done = bf16[1,1152,1152]{2,1,0:T(8,128)(2,1)} async-done(((bf16[1,144,1152]{2,1,0:T(8,128)(2,1)}), bf16[1,1152,1152]{2,1,0:T(8,128)(2,1)}) %all-gather.19.cloned.1.call-update) | async-done | bytes 2654224 | tf_op jit(solution)/shard_map/all_gather | solution.py:33
  129.0 1.7 copy-done.8
  133.9 4.6 %collective-permute-start = (bf16[128,1152]{1,0:T(8,128)(2,1)S(1)}, bf16[128,1152]{1,0:T(8,128)(2,1)S(1)}, u32[]{:S(2)}, u32[]{:S(2)}) collective-permute-start(bf16[128,1152]{1,0:T(8,128)(2,1)S(1)} %add_convert_fusion.1), channel_id=1, source_target_pairs={{0,2},{2,4},{4,6},{1,3},{3,5},{5,7},{8,10},{10,12},{12,14},{9,11},... | collective-permute-start | bytes 884744 | tf_op jit(solution)/shard_map/ppermute | solution.py:144
  138.9 4.8 %collective-permute-done.1 = bf16[128,1152]{1,0:T(8,128)(2,1)S(1)} collective-permute-done((bf16[128,1152]{1,0:T(8,128)(2,1)S(1)}, bf16[128,1152]{1,0:T(8,128)(2,1)S(1)}, u32[]{:S(2)}, u32[]{:S(2)}) %collective-permute-start.1) | collective-permute-done | bytes 294944 | tf_op jit(solution)/shard_map/ppermute | solution.py:145
  145.0 4.6 %collective-permute-start.4 = (bf16[128,1152]{1,0:T(8,128)(2,1)S(1)}, bf16[128,1152]{1,0:T(8,128)(2,1)S(1)}, u32[]{:S(2)}, u32[]{:S(2)}) collective-permute-start(bf16[128,1152]{1,0:T(8,128)(2,1)S(1)} %collective-permute-done), channel_id=1, source_target_pairs={{0,2},{2,4},{4,6},{1,3},{3,5},{5,7},{8,10},{10,12},{12,14},{9,11},... | collective-permute-start | bytes 884744 | tf_op jit(solution)/shard_map/ppermute | solution.py:144
  151.0 3.0 %collective-permute-done.2 = bf16[128,1152]{1,0:T(8,128)(2,1)S(1)} collective-permute-done((bf16[128,1152]{1,0:T(8,128)(2,1)S(1)}, bf16[128,1152]{1,0:T(8,128)(2,1)S(1)}, u32[]{:S(2)}, u32[]{:S(2)}) %collective-permute-start.2) | collective-permute-done | bytes 294944 | tf_op jit(solution)/shard_map/ppermute | solution.py:145
  155.3 4.8 %collective-permute-start.5 = (bf16[128,1152]{1,0:T(8,128)(2,1)S(1)}, bf16[128,1152]{1,0:T(8,128)(2,1)S(1)}, u32[]{:S(2)}, u32[]{:S(2)}) collective-permute-start(bf16[128,1152]{1,0:T(8,128)(2,1)S(1)} %collective-permute-done.4), channel_id=1, source_target_pairs={{0,2},{2,4},{4,6},{1,3},{3,5},{5,7},{8,10},{10,12},{12,14},{9,11},... | collective-permute-start | bytes 884744 | tf_op jit(solution)/shard_map/ppermute | solution.py:144
  160.2 3.4 %collective-permute-done.3 = bf16[128,1152]{1,0:T(8,128)(2,1)S(1)} collective-permute-done((bf16[128,1152]{1,0:T(8,128)(2,1)S(1)}, bf16[128,1152]{1,0:T(8,128)(2,1)S(1)}, u32[]{:S(2)}, u32[]{:S(2)}) %collective-permute-start.3) | collective-permute-done | bytes 294944 | tf_op jit(solution)/shard_map/ppermute | solution.py:145
  167.3 1.7 copy-done.9
  170.5 1.7 copy.89
  178.0 1.9 select_reduce_fusion
  179.9 2.0 fusion.1
  183.8 2.2 fusion.7
  188.3 5.6 %all-to-all-start = ((bf16[4,128,288]{1,2,0:T(8,128)(2,1)}), bf16[4,128,288]{1,2,0:T(8,128)(2,1)S(1)}, u32[]{:S(2)}, u32[]{:S(2)}) async-start(bf16[4,128,288]{1,2,0:T(8,128)(2,1)} %gather_fusion.2), calls=%async_computation | async-start | bytes 589824 | tf_op jit(solution)/shard_map/all_to_all | solution.py:161
  195.8 5.0 %all-to-all-done = bf16[4,128,288]{1,2,0:T(8,128)(2,1)S(1)} async-done(((bf16[4,128,288]{1,2,0:T(8,128)(2,1)}), bf16[4,128,288]{1,2,0:T(8,128)(2,1)S(1)}, u32[]{:S(2)}, u32[]{:S(2)}) %all-to-all-start) | async-done | bytes 294944 | tf_op jit(solution)/shard_map/all_to_all | solution.py:161
  201.1 1.9 copy-done.6
  205.5 3.7 %all-to-all-start.1 = ((bf16[1,2,64,1152]{3,1,0,2:T(2,128)(2,1)}), bf16[1,2,64,1152]{3,1,0,2:T(2,128)(2,1)S(1)}, u32[]{:S(2)}, u32[]{:S(2)}) async-start(bf16[1,2,64,1152]{3,1,0,2:T(2,128)(2,1)} %copy.96), calls=%async_computation.1 | async-start | bytes 589824 | tf_op jit(solution)/shard_map/all_to_all | solution.py:166
  209.3 7.3 %all-to-all-done.1 = bf16[1,2,64,1152]{3,1,0,2:T(2,128)(2,1)S(1)} async-done(((bf16[1,2,64,1152]{3,1,0,2:T(2,128)(2,1)}), bf16[1,2,64,1152]{3,1,0,2:T(2,128)(2,1)S(1)}, u32[]{:S(2)}, u32[]{:S(2)}) %all-to-all-start.1) | async-done | bytes 294944 | tf_op jit(solution)/shard_map/all_to_all | solution.py:166
  217.4 29.7 %all-gather.25.cloned.1.call-done = bf16[1,1152,3456]{2,1,0:T(8,128)(2,1)} async-done(((bf16[1,144,3456]{2,1,0:T(8,128)(2,1)}), bf16[1,1152,3456]{2,1,0:T(8,128)(2,1)}) %all-gather.25.cloned.1.call-update) | async-done | bytes 7962640 | tf_op jit(solution)/shard_map/all_gather | solution.py:33
  247.1 3.3 %copy-done.2 = bf16[1,1152,3456]{2,1,0:T(8,128)(2,1)S(1)} copy-done((bf16[1,1152,3456]{2,1,0:T(8,128)(2,1)S(1)}, bf16[1,1152,3456]{2,1,0:T(8,128)(2,1)}, u32[]{:S(2)}) %copy-start.2) | copy-done | bytes 7962648
  250.4 3.9 %shard_map.150 = f32[128,3456]{1,0:T(8,128)S(1)} custom-call(bf16[128,1152]{1,0:T(8,128)(2,1)S(1)} %fusion.18.x_ref, bf16[1152,3456]{1,0:T(8,128)(2,1)S(1)} %bitcast.180), custom_call_target="tpu_custom_call" | custom-call | flops 1019215872 | bytes 10027008 | tf_op jit(solution)/shard_map/pallas_call | solution.py:50
  257.5 21.9 %all-gather.27.cloned.1.call-done = bf16[1,1152,1152]{2,1,0:T(8,128)(2,1)} async-done(((bf16[1,144,1152]{2,1,0:T(8,128)(2,1)}), bf16[1,1152,1152]{2,1,0:T(8,128)(2,1)}) %all-gather.27.cloned.1.call-update) | async-done | bytes 2654224 | tf_op jit(solution)/shard_map/all_gather | solution.py:33
  279.3 1.9 copy-done.5
  (177 shorter events, 51.7 us)
Async XLA Ops:
  6.5 2.7 copy-start.14
  6.5 58.1 %all-gather.15.cloned.1.call-start = ((), (), s32[]{:S(2)}) async-start(), calls=%async_computation.2 | async-start | bytes 8957952 | tf_op jit(solution)/shard_map/all_gather | solution.py:33
  8.1 2.0 copy-start.15
  9.2 87.6 %all-gather.17.cloned.1.call-start = ((), (), s32[]{:S(2)}) async-start(), calls=%async_computation.3 | async-start | bytes 2985984 | tf_op jit(solution)/shard_map/all_gather | solution.py:33
  10.1 118.9 %all-gather.19.cloned.1.call-start = ((), (), s32[]{:S(2)}) async-start(), calls=%async_computation.4 | async-start | bytes 2985984 | tf_op jit(solution)/shard_map/all_gather | solution.py:33
  10.9 155.1 %all-gather.21.cloned.1.call-start = ((), (), s32[]{:S(2)}) async-start(), calls=%async_computation.5 | async-start | bytes 2322432 | tf_op jit(solution)/shard_map/all_gather | solution.py:33
  20.3 180.8 %all-gather.23.cloned.1.call-start = ((), (), s32[]{:S(2)}) async-start(), calls=%async_computation.6 | async-start | bytes 2985984 | tf_op jit(solution)/shard_map/all_gather | solution.py:33
  21.2 2.7 copy-start.17
  21.2 226.0 %all-gather.25.cloned.1.call-start = ((), (), s32[]{:S(2)}) async-start(), calls=%async_computation.7 | async-start | bytes 8957952 | tf_op jit(solution)/shard_map/all_gather | solution.py:33
  21.2 3.4 %copy-start.10 = (bf16[1,2,64,1152]{3,2,1,0:T(8,128)(2,1)S(1)}, bf16[1,2,64,1152]{3,2,1,0:T(8,128)(2,1)}, u32[]{:S(2)}) copy-start(bf16[1,2,64,1152]{3,2,1,0:T(8,128)(2,1)} %param.15) | copy-start | bytes 884740
  21.2 3.4 %copy-start.13 = (bf16[1,2,64,1152]{3,2,1,0:T(8,128)(2,1)S(1)}, bf16[1,2,64,1152]{3,2,1,0:T(8,128)(2,1)}, u32[]{:S(2)}) copy-start(bf16[1,2,64,1152]{3,2,1,0:T(8,128)(2,1)} %param.16) | copy-start | bytes 884740
  23.6 1.8 copy-start.22
  23.6 2.4 copy-start.20
  23.7 255.7 %all-gather.27.cloned.1.call-start = ((), (), s32[]{:S(2)}) async-start(), calls=%async_computation.8 | async-start | bytes 2985984 | tf_op jit(solution)/shard_map/all_gather | solution.py:33
  64.7 3.3 %copy-start.3 = (bf16[1,1152,3456]{2,1,0:T(8,128)(2,1)S(1)}, bf16[1,1152,3456]{2,1,0:T(8,128)(2,1)}, u32[]{:S(2)}) copy-start(bf16[1,1152,3456]{2,1,0:T(8,128)(2,1)} %all-gather.15.cloned.1.call-done) | copy-start | bytes 23887876
  96.8 1.7 copy-start.7
  129.0 1.7 copy-start.8
  132.6 11.1 %collective-permute-start.1 = (bf16[128,1152]{1,0:T(8,128)(2,1)S(1)}, bf16[128,1152]{1,0:T(8,128)(2,1)S(1)}, u32[]{:S(2)}, u32[]{:S(2)}) collective-permute-start(bf16[128,1152]{1,0:T(8,128)(2,1)S(1)} %add_convert_fusion.1), channel_id=1, source_target_pairs={{2,0},{4,2},{6,4},{3,1},{5,3},{7,5},{10,8},{12,10},{14,12},{11,9},... | collective-permute-start | bytes 884744 | tf_op jit(solution)/shard_map/ppermute | solution.py:145
  133.9 11.1 %collective-permute-start = (bf16[128,1152]{1,0:T(8,128)(2,1)S(1)}, bf16[128,1152]{1,0:T(8,128)(2,1)S(1)}, u32[]{:S(2)}, u32[]{:S(2)}) collective-permute-start(bf16[128,1152]{1,0:T(8,128)(2,1)S(1)} %add_convert_fusion.1), channel_id=1, source_target_pairs={{0,2},{2,4},{4,6},{1,3},{3,5},{5,7},{8,10},{10,12},{12,14},{9,11},... | collective-permute-start | bytes 884744 | tf_op jit(solution)/shard_map/ppermute | solution.py:144
  143.7 10.3 %collective-permute-start.2 = (bf16[128,1152]{1,0:T(8,128)(2,1)S(1)}, bf16[128,1152]{1,0:T(8,128)(2,1)S(1)}, u32[]{:S(2)}, u32[]{:S(2)}) collective-permute-start(bf16[128,1152]{1,0:T(8,128)(2,1)S(1)} %collective-permute-done.1), channel_id=1, source_target_pairs={{2,0},{4,2},{6,4},{3,1},{5,3},{7,5},{10,8},{12,10},{14,12},{11,9},... | collective-permute-start | bytes 884744 | tf_op jit(solution)/shard_map/ppermute | solution.py:145
  145.0 10.3 %collective-permute-start.4 = (bf16[128,1152]{1,0:T(8,128)(2,1)S(1)}, bf16[128,1152]{1,0:T(8,128)(2,1)S(1)}, u32[]{:S(2)}, u32[]{:S(2)}) collective-permute-start(bf16[128,1152]{1,0:T(8,128)(2,1)S(1)} %collective-permute-done), channel_id=1, source_target_pairs={{0,2},{2,4},{4,6},{1,3},{3,5},{5,7},{8,10},{10,12},{12,14},{9,11},... | collective-permute-start | bytes 884744 | tf_op jit(solution)/shard_map/ppermute | solution.py:144
  154.0 9.5 %collective-permute-start.3 = (bf16[128,1152]{1,0:T(8,128)(2,1)S(1)}, bf16[128,1152]{1,0:T(8,128)(2,1)S(1)}, u32[]{:S(2)}, u32[]{:S(2)}) collective-permute-start(bf16[128,1152]{1,0:T(8,128)(2,1)S(1)} %collective-permute-done.2), channel_id=1, source_target_pairs={{2,0},{4,2},{6,4},{3,1},{5,3},{7,5},{10,8},{12,10},{14,12},{11,9},... | collective-permute-start | bytes 884744 | tf_op jit(solution)/shard_map/ppermute | solution.py:145
  155.3 9.4 %collective-permute-start.5 = (bf16[128,1152]{1,0:T(8,128)(2,1)S(1)}, bf16[128,1152]{1,0:T(8,128)(2,1)S(1)}, u32[]{:S(2)}, u32[]{:S(2)}) collective-permute-start(bf16[128,1152]{1,0:T(8,128)(2,1)S(1)} %collective-permute-done.4), channel_id=1, source_target_pairs={{0,2},{2,4},{4,6},{1,3},{3,5},{5,7},{8,10},{10,12},{12,14},{9,11},... | collective-permute-start | bytes 884744 | tf_op jit(solution)/shard_map/ppermute | solution.py:144
  186.2 7.6 %copy-start.24 = (s32[4]{0:T(128)S(1)}, s32[4]{0:T(128)}, u32[]{:S(2)}) copy-start(s32[4]{0:T(128)} %param.18) | copy-start | bytes 52
  186.2 9.0 %copy-start.21 = (f32[3,1152]{1,0:T(4,128)S(1)}, f32[3,1152]{1,0:T(4,128)}, u32[]{:S(2)}) copy-start(f32[3,1152]{1,0:T(4,128)} %param.28) | copy-start | bytes 41476
  188.3 12.6 %all-to-all-start = ((bf16[4,128,288]{1,2,0:T(8,128)(2,1)}), bf16[4,128,288]{1,2,0:T(8,128)(2,1)S(1)}, u32[]{:S(2)}, u32[]{:S(2)}) async-start(bf16[4,128,288]{1,2,0:T(8,128)(2,1)} %gather_fusion.2), calls=%async_computation | async-start | bytes 589824 | tf_op jit(solution)/shard_map/all_to_all | solution.py:161
  201.1 1.9 copy-start.6
  205.5 11.1 %all-to-all-start.1 = ((bf16[1,2,64,1152]{3,1,0,2:T(2,128)(2,1)}), bf16[1,2,64,1152]{3,1,0,2:T(2,128)(2,1)S(1)}, u32[]{:S(2)}, u32[]{:S(2)}) async-start(bf16[1,2,64,1152]{3,1,0,2:T(2,128)(2,1)} %copy.96), calls=%async_computation.1 | async-start | bytes 589824 | tf_op jit(solution)/shard_map/all_to_all | solution.py:166
  217.2 30.0 %copy-start.11 = (f32[1,4,2,16,1152]{4,3,2,1,0:T(8,128)}, f32[1,4,2,16,1152]{4,3,2,1,0:T(8,128)S(1)}, u32[]{:S(2)}) copy-start(f32[1,4,2,16,1152]{4,3,2,1,0:T(8,128)S(1)} %copy.98) | copy-start | bytes 1769476
  247.1 3.3 %copy-start.2 = (bf16[1,1152,3456]{2,1,0:T(8,128)(2,1)S(1)}, bf16[1,1152,3456]{2,1,0:T(8,128)(2,1)}, u32[]{:S(2)}) copy-start(bf16[1,1152,3456]{2,1,0:T(8,128)(2,1)} %all-gather.25.cloned.1.call-done) | copy-start | bytes 23887876
  279.3 4.0 %copy-start.1 = (bf16[288,3456]{1,0:T(8,128)(2,1)S(1)}, bf16[288,3456]{1,0:T(8,128)(2,1)}, u32[]{:S(2)}) copy-start(bf16[288,3456]{1,0:T(8,128)(2,1)} %param.19) | copy-start | bytes 5971972
  279.3 1.9 copy-start.5
  (8 other events, 11.7 us)
Sparse Core Ops, SparseCore 0:
  9.3 55.2 all-gather.14
  66.5 30.2 all-gather.16
  98.7 30.2 all-gather.18
  130.7 27.7 all-gather.20
  160.3 30.2 all-gather.22
  192.3 54.7 all-gather.24
  249.0 30.2 all-gather.26
where the time goes:
time: 291 us; the launch traced here: 290 us
  waiting for transfers between devices  159 us (55%)
  local copies, waits for them, and re-layouts  55.2 us (19%)
  starting transfers between devices  27.5 us (9%)
  Pallas kernels  14.5 us (5%)
  between operations  14.2 us (5%)
  other arithmetic  12.7 us (4%)
  matrix products  6.82 us (2%)
    all_gather x7, waiting for transfers between devices, collect_rows(): return lax.all_gather(own_share, ('seq', 'dp'), axis=0, tiled=True)  134 us
    unnamed x50, local copies, waits for them, and re-layouts  18.4 us
    pallas_call x7, Pallas kernels, project(): pl.pallas_call(matmul_kernel, grid=(rows // row_tile, columns // column_t...  14.5 us
    ppermute x3, starting transfers between devices, per_device(): lax.ppermute(upward[-1], 'view', [(i, i + 1) for i in range(view_size - 1)])  13.9 us
    ppermute x3, waiting for transfers between devices, per_device(): lax.ppermute(downward[-1], 'view', [(i + 1, i) for i in range(view_size -...  11.3 us
    all_to_all x1, waiting for transfers between devices, per_device(): lax.all_to_all(spaced, 'seq', split_axis=2, concat_axis=1, tiled=True)  7.29 us
    dynamic_slice x7, local copies, waits for them, and re-layouts, collect_rows(): lax.dynamic_index_in_dim(shares, lax.axis_index('dp'), 0, keepdims=False)  7.23 us
  transfers between devices with their start and end apart: 15, of which 11 were waited for; matrix products, arithmetic and copies ran while one was open for 19% of the time, Pallas kernels for 5%

commit v1 on v0

--- a/solution.py
+++ b/solution.py
@@ -1,3 +1,5 @@
+import math
+
 import jax
 import jax.numpy as jnp
 from jax import lax
@@ -33,6 +35,20 @@
     return lax.all_gather(own_share, ("seq", "dp"), axis=0, tiled=True)
 
 
+def pass_rows(weight, seq_size):
+    pieces = [weight]
+    for k in range(1, seq_size):
+        pieces.append(lax.ppermute(weight, "seq", [(i, (i + k) % seq_size) for i in range(seq_size)]))
+    order = (lax.axis_index("seq") - jnp.arange(seq_size)) % seq_size
+    return jnp.concatenate(pieces, axis=0), order
+
+
+def project_passed(inputs, passed):
+    weight, order = passed
+    chunks = inputs.reshape(inputs.shape[0], order.shape[0], -1)
+    return project(jnp.take(chunks, order, axis=1, mode="clip").reshape(inputs.shape), weight)
+
+
 def tile_of(size, unit, largest):
     tiles = [t for t in range(unit, min(size, largest) + 1, unit) if size % t == 0]
     return tiles[-1] if tiles else size
@@ -42,17 +58,18 @@
     out_ref[...] = jnp.dot(x_ref[...], w_ref[...], preferred_element_type=jnp.float32)
 
 
-def project(inputs, weight):
+def project(inputs, weight, first=0, columns=None):
     rows, depth = inputs.shape
-    columns = weight.shape[1]
+    columns = columns or weight.shape[1]
     row_tile = tile_of(rows, 16, 1024)
-    column_tile = tile_of(columns, 128, 512)
+    column_tile = tile_of(math.gcd(columns, first), 128, 512)
+    skipped = first // column_tile
     return pl.pallas_call(
         matmul_kernel,
         grid=(rows // row_tile, columns // column_tile),
         in_specs=[
             pl.BlockSpec((row_tile, depth), lambda i, j: (i, 0)),
-            pl.BlockSpec((depth, column_tile), lambda i, j: (0, j)),
+            pl.BlockSpec((depth, column_tile), lambda i, j: (0, j + skipped)),
         ],
         out_specs=pl.BlockSpec((row_tile, column_tile), lambda i, j: (i, j)),
         out_shape=jax.ShapeDtypeStruct((rows, columns), jnp.float32),
@@ -93,6 +110,7 @@
 
 
 def per_device(
+    seq_size,
     view_size,
     dp_size,
     latent,
@@ -118,15 +136,13 @@
     view_heads = HEADS // view_size
     collect = lambda weight: collect_rows(weight, dp_size)
 
+    out_ctrl = pass_rows(w_out_ctrl, seq_size)
+    join = pass_rows(w_join, seq_size)
     qkv_ctrl = collect(w_qkv_ctrl)
-    out_ctrl = collect(w_out_ctrl)
-    join = collect(w_join)
     columns = w_qkv_space.reshape(-1, 3, view_size, width // view_size)
     columns = lax.dynamic_index_in_dim(columns, view, 2, keepdims=False)
-    qkv_space = collect(columns.reshape(-1, 3 * width // view_size))
-    out_space = collect(w_out_space)
-    qkv_time = collect(w_qkv_time)
-    out_time = collect(w_out_time)
+    space = collect(jnp.concatenate([w_out_space, columns.reshape(-1, 3 * width // view_size)], axis=1))
+    time = collect(jnp.concatenate([w_qkv_time, w_out_time], axis=1))
 
     base = latent.reshape(tokens, width).astype(jnp.float32)
     ctrl_in = base + condition.reshape(tokens, width).astype(jnp.float32)
@@ -135,8 +151,8 @@
     by_frame = [part.reshape(HEADS * frames_here, patches, head_size) for part in parts]
     attended = attend(*by_frame, None).reshape(HEADS, tokens, head_size)
     flat = attended.transpose(1, 0, 2).reshape(tokens, width)
-    control = (ctrl_in + mod_ctrl[2] * project(flat, out_ctrl)).astype(jnp.bfloat16)
-    joined = base + project(control, join)
+    control = (ctrl_in + mod_ctrl[2] * project_passed(flat, out_ctrl)).astype(jnp.bfloat16)
+    joined = base + project_passed(control, join)
 
     normed = modulate(joined, mod_space)
     upward, downward = [normed], [normed]
@@ -146,7 +162,7 @@
     everyone = [normed] + [jnp.where(view >= t, upward[t], downward[view_size - t]) for t in range(1, view_size)]
     cameras = (view - jnp.arange(view_size)) % view_size
     everyone = jnp.stack(everyone).reshape(view_size * tokens, width)
-    packed = project(everyone, qkv_space)
+    packed = project(everyone, space[:, width:])
     parts = heads_of(packed, qk_gain[1], view_heads)
     by_frame = [
         part.reshape(view_heads, view_size, frames_here, patches, head_size)
@@ -160,13 +176,13 @@
     attended = attended.transpose(2, 1, 3, 0, 4).reshape(view_size, tokens, width // view_size)
     attended = lax.all_to_all(attended[cameras], "view", split_axis=0, concat_axis=0, tiled=True)
     flat = attended.transpose(1, 0, 2).reshape(tokens, width)
-    spaced = (joined + mod_space[2] * project(flat, out_space)).astype(jnp.bfloat16)
+    spaced = (joined + mod_space[2] * project(flat, space, 0, width)).astype(jnp.bfloat16)
 
     spaced = spaced.reshape(1, frames_here, patches, width)
     patched = lax.all_to_all(spaced, "seq", split_axis=2, concat_axis=1, tiled=True)
     frames, patch_here = patched.shape[1:3]
     stream = patched.reshape(frames * patch_here, width).astype(jnp.float32)
-    packed = project(modulate(stream, mod_time), qkv_time)
+    packed = project(modulate(stream, mod_time), time, 0, 3 * width)
     parts = heads_of(packed, qk_gain[2], HEADS)
     own_live = lax.dynamic_index_in_dim(live_frames, view, 0, keepdims=False)
     place = jnp.arange(frames * patch_here, dtype=jnp.int32)
@@ -174,7 +190,7 @@
     alive = place[None, :] // patch_here < own_live
     attended = attend(*parts, same & alive)
     flat = attended.transpose(1, 0, 2).reshape(frames * patch_here, width)
-    result = stream + mod_time[2] * project(flat, out_time)
+    result = stream + mod_time[2] * project(flat, time, 3 * width, width)
     return result.astype(jnp.bfloat16).reshape(patched.shape)
 
 
@@ -196,7 +212,7 @@
         P("dp", None),
         P(),
     )
-    sizes = mesh.shape["view"], mesh.shape["dp"]
+    sizes = mesh.shape["seq"], mesh.shape["view"], mesh.shape["dp"]
 
     def run(*arrays):
         return per_device(*sizes, *arrays)

time: 291 us -> 270 us (0.928)
  waiting for transfers between devices: 159 us -> 108 us
  other arithmetic: 12.7 us -> 26.5 us
  local copies, waits for them, and re-layouts: 55.2 us -> 67.6 us
  starting transfers between devices: 27.5 us -> 32.1 us
    all_gather x7 -> x3, waiting for transfers between devices: 134 us -> 0.04 us  [collect_rows(): return lax.all_gather(own_share, ('seq', 'dp'), axis=0, tiled=True)]
    ppermute x0 -> x6, waiting for transfers between devices: none -> 80.2 us  [pass_rows(): lax.ppermute(weight, 'seq', [(i, (i + k) % seq_size) for i in range(seq_s...]
    concatenate x0 -> x4, other arithmetic: none -> 8.69 us  [the longest x2 6.43 us: pass_rows(): return (jnp.concatenate(pieces, axis=0), order)]
    dynamic_slice x7 -> x2, local copies, waits for them, and re-layouts: 7.23 us -> 2.19 us  [collect_rows(): lax.dynamic_index_in_dim(shares, lax.axis_index('dp'), 0, keepdims=False)]
    ppermute x0 -> x6, starting transfers between devices: none -> 4.98 us  [pass_rows(): lax.ppermute(weight, 'seq', [(i, (i + k) % seq_size) for i in range(seq_s...]
    unnamed x50 -> x70, local copies, waits for them, and re-layouts: 18.4 us -> 19.9 us
  transfers between devices with their start and end apart: 15 -> 17, of which waited for: 11 -> 14; matrix products, arithmetic and copies ran while one was open for 19% -> 28% of each run, Pallas kernels for 5% -> 4%
where the time goes in v1:
time: 270 us; the launch traced here: 269 us
  waiting for transfers between devices  108 us (40%)
  local copies, waits for them, and re-layouts  67.6 us (25%)
  starting transfers between devices  32.1 us (12%)
  other arithmetic  26.5 us (10%)
  Pallas kernels  14.8 us (5%)
  between operations  14 us (5%)
  matrix products  6.53 us (2%)
    ppermute x6, waiting for transfers between devices, pass_rows(): lax.ppermute(weight, 'seq', [(i, (i + k) % seq_size) for i in range(seq_s...  80.2 us
    unnamed x70, local copies, waits for them, and re-layouts  19.9 us
    pallas_call x7, Pallas kernels, project(): pl.pallas_call(matmul_kernel, grid=(rows // row_tile, columns // column_t...  14.8 us
    ppermute x3, starting transfers between devices, per_device(): lax.ppermute(upward[-1], 'view', [(i, i + 1) for i in range(view_size - 1)])  13.6 us
    ppermute x3, waiting for transfers between devices, per_device(): lax.ppermute(downward[-1], 'view', [(i + 1, i) for i in range(view_size -...  11.3 us
    all_to_all x1, waiting for transfers between devices, per_device(): lax.all_to_all(attended[cameras], 'view', split_axis=0, concat_axis=0, ti...  7.49 us
    concatenate x2, other arithmetic, pass_rows(): return (jnp.concatenate(pieces, axis=0), order)  6.43 us
    all_to_all x1, waiting for transfers between devices, per_device(): lax.all_to_all(spaced, 'seq', split_axis=2, concat_axis=1, tiled=True)  5.99 us
  transfers between devices with their start and end apart: 17, of which 14 were waited for; matrix products, arithmetic and copies ran while one was open for 28% of the time, Pallas kernels for 4%

profile of v1, /device:TPU:0, one launch (start us, length us, event | category | flops | bytes accessed | tf_op | source)
XLA Modules:
  0.0 269.0 jit_solution(3948279791549815974)
XLA Ops:
  9.2 3.5 %reshape.490 = bf16[288,3,4,288]{3,2,1,0:T(4,128)(2,1)S(1)} reshape(bf16[288,3456]{1,0:T(8,128)(2,1)} %param.22) | data formatting | bytes 3981312 | tf_op jit(solution)/shard_map/reshape | solution.py:142
  12.7 4.6 %dynamic-slice_reduce_fusion = bf16[288,3,288]{2,1,0:T(4,128)(2,1)S(1)} fusion(bf16[288,3,4,288]{3,2,1,0:T(4,128)(2,1)S(1)} %reshape.490, s32[]{:T(128)S(6)} %select_n.121), kind=kLoop, calls=%fused_computation.17 | loop fusion | bytes 995332 | tf_op jit(solution)/shard_map/jit(dynamic_index_in_dim)/dynamic_slice | solution.py:143
  17.8 2.1 fusion.15
  22.0 2.6 collective-permute-start.1
  30.2 16.8 %collective-permute-done = bf16[288,1152]{1,0:T(8,128)(2,1)S(1)} collective-permute-done((bf16[288,1152]{1,0:T(8,128)(2,1)S(1)}, bf16[288,1152]{1,0:T(8,128)(2,1)S(1)}, u32[]{:S(2)}, u32[]{:S(2)}) %collective-permute-start) | collective-permute-done | bytes 663584 | tf_op jit(solution)/shard_map/ppermute | solution.py:41
  47.7 26.0 %collective-permute-done.2 = bf16[288,1152]{1,0:T(8,128)(2,1)} collective-permute-done((bf16[288,1152]{1,0:T(8,128)(2,1)S(1)}, bf16[288,1152]{1,0:T(8,128)(2,1)}, u32[]{:S(2)}, u32[]{:S(2)}) %collective-permute-start.2) | collective-permute-done | bytes 663584 | tf_op jit(solution)/shard_map/ppermute | solution.py:41
  73.7 4.9 %pad_maximum_fusion.w_ref = bf16[1152,1152]{1,0:T(8,128)(2,1)} fusion(bf16[288,1152]{1,0:T(8,128)(2,1)} %collective-permute-done.2, bf16[288,1152]{1,0:T(8,128)(2,1)} %collective-permute-done.1, bf16[288,1152]{1,0:T(8,128)(2,1)S(1)} %collective-permute-done, bf16[288,1152]{1,0:T(8,128)(2,1)S(1)} %copy-done.17), kind=kLoop, calls=%fused_computation.6 | loop fusion | flops 10616832 | bytes 5308416 | tf_op jit(solution)/shard_map/concatenate | solution.py:43
  78.6 18.1 %collective-permute-done.3 = bf16[288,1152]{1,0:T(8,128)(2,1)S(1)} collective-permute-done((bf16[288,1152]{1,0:T(8,128)(2,1)S(1)}, bf16[288,1152]{1,0:T(8,128)(2,1)S(1)}, u32[]{:S(2)}, u32[]{:S(2)}) %collective-permute-start.3) | collective-permute-done | bytes 663584 | tf_op jit(solution)/shard_map/ppermute | solution.py:41
  97.6 17.9 %collective-permute-done.5 = bf16[288,1152]{1,0:T(8,128)(2,1)S(1)} collective-permute-done((bf16[288,1152]{1,0:T(8,128)(2,1)S(1)}, bf16[288,1152]{1,0:T(8,128)(2,1)S(1)}, u32[]{:S(2)}, u32[]{:S(2)}) %collective-permute-start.5) | collective-permute-done | bytes 663584 | tf_op jit(solution)/shard_map/ppermute | solution.py:41
  117.0 3.3 %copy-done.6 = bf16[1,1152,3456]{2,1,0:T(8,128)(2,1)S(1)} copy-done((bf16[1,1152,3456]{2,1,0:T(8,128)(2,1)S(1)}, bf16[1,1152,3456]{2,1,0:T(8,128)(2,1)}, u32[]{:S(2)}) %copy-start.6) | copy-done | bytes 7962648
  120.2 3.9 %shard_map.145 = f32[128,3456]{1,0:T(8,128)S(1)} custom-call(bf16[128,1152]{1,0:T(8,128)(2,1)S(1)} %add_convert_fusion.3.x_ref, bf16[1152,3456]{1,0:T(8,128)(2,1)S(1)} %bitcast.186), custom_call_target="tpu_custom_call" | custom-call | flops 1019215872 | bytes 10027008 | tf_op jit(solution)/shard_map/pallas_call | solution.py:67
  125.4 2.7 %copy.80 = f32[128,3456]{0,1:T(8,128)} copy(f32[128,3456]{1,0:T(8,128)} %copy-done.7) | data formatting | bytes 3538944 | tf_op jit(solution)/shard_map/pallas_call | solution.py:67
  129.2 2.8 %multiply_reduce_fusion.7 = (f32[16,128]{1,0:T(8,128)S(1)}, f32[16,128]{1,0:T(8,128)}, f32[1,16,128,72]{2,3,1,0:T(8,128)S(1)}, f32[1,16,128,72]{2,3,1,0:T(8,128)}) fusion(f32[3,16,128,72]{2,3,1,0:T(8,128)} %bitcast.193), kind=kLoop, calls=%fused_computation.69 | loop fusion | flops 585728 | bytes 2375680 | tf_op jit(solution)/shard_map/reduce_sum | solution.py:28
  132.9 2.4 squeeze.46
  135.3 2.0 copy.82
  137.3 2.3 squeeze.47
  144.7 2.0 multiply_convert_fusion.2
  148.5 3.3 %fusion.5 = bf16[32,64,72]{2,1,0:T(8,128)(2,1)} fusion(bf16[32,64,72]{2,1,0:T(8,128)(2,1)} %bitcast.211, f32[32,64]{1,0:T(8,128)S(1)} %fusion.57, f32[32,64,64]{1,2,0:T(8,128)} %copy-done.15), kind=kOutput, calls=%fused_computation.18 | convolution fusion | flops 19433536 | bytes 1122304 | tf_op jit(solution)/shard_map/bqk,bkd->bqd/dot_general | solution.py:100
  165.0 4.6 %collective-permute-start.6 = (bf16[128,1152]{1,0:T(8,128)(2,1)S(1)}, bf16[128,1152]{1,0:T(8,128)(2,1)S(1)}, u32[]{:S(2)}, u32[]{:S(2)}) collective-permute-start(bf16[128,1152]{1,0:T(8,128)(2,1)S(1)} %add_convert_fusion.1), channel_id=1, source_target_pairs={{0,2},{2,4},{4,6},{1,3},{3,5},{5,7},{8,10},{10,12},{12,14},{9,11},... | collective-permute-start | bytes 884744 | tf_op jit(solution)/shard_map/ppermute | solution.py:160
  170.0 4.3 %collective-permute-done.7 = bf16[128,1152]{1,0:T(8,128)(2,1)S(1)} collective-permute-done((bf16[128,1152]{1,0:T(8,128)(2,1)S(1)}, bf16[128,1152]{1,0:T(8,128)(2,1)S(1)}, u32[]{:S(2)}, u32[]{:S(2)}) %collective-permute-start.7) | collective-permute-done | bytes 294944 | tf_op jit(solution)/shard_map/ppermute | solution.py:161
  176.0 4.4 %collective-permute-start.10 = (bf16[128,1152]{1,0:T(8,128)(2,1)S(1)}, bf16[128,1152]{1,0:T(8,128)(2,1)S(1)}, u32[]{:S(2)}, u32[]{:S(2)}) collective-permute-start(bf16[128,1152]{1,0:T(8,128)(2,1)S(1)} %collective-permute-done.6), channel_id=1, source_target_pairs={{0,2},{2,4},{4,6},{1,3},{3,5},{5,7},{8,10},{10,12},{12,14},{9,11},... | collective-permute-start | bytes 884744 | tf_op jit(solution)/shard_map/ppermute | solution.py:160
  183.7 2.0 collective-permute-done.8
  187.7 4.6 %collective-permute-start.11 = (bf16[128,1152]{1,0:T(8,128)(2,1)S(1)}, bf16[128,1152]{1,0:T(8,128)(2,1)S(1)}, u32[]{:S(2)}, u32[]{:S(2)}) collective-permute-start(bf16[128,1152]{1,0:T(8,128)(2,1)S(1)} %collective-permute-done.10), channel_id=1, source_target_pairs={{0,2},{2,4},{4,6},{1,3},{3,5},{5,7},{8,10},{10,12},{12,14},{9,11},... | collective-permute-start | bytes 884744 | tf_op jit(solution)/shard_map/ppermute | solution.py:160
  192.3 5.0 %collective-permute-done.9 = bf16[128,1152]{1,0:T(8,128)(2,1)S(1)} collective-permute-done((bf16[128,1152]{1,0:T(8,128)(2,1)S(1)}, bf16[128,1152]{1,0:T(8,128)(2,1)S(1)}, u32[]{:S(2)}, u32[]{:S(2)}) %collective-permute-start.9) | collective-permute-done | bytes 294944 | tf_op jit(solution)/shard_map/ppermute | solution.py:161
  213.7 5.9 %all-to-all-start = ((bf16[4,128,288]{1,2,0:T(8,128)(2,1)}), bf16[4,128,288]{1,2,0:T(8,128)(2,1)S(1)}, u32[]{:S(2)}, u32[]{:S(2)}) async-start(bf16[4,128,288]{1,2,0:T(8,128)(2,1)} %gather_fusion.4), calls=%async_computation | async-start | bytes 589824 | tf_op jit(solution)/shard_map/all_to_all | solution.py:177
  221.3 7.5 %all-to-all-done = bf16[4,128,288]{1,2,0:T(8,128)(2,1)S(1)} async-done(((bf16[4,128,288]{1,2,0:T(8,128)(2,1)}), bf16[4,128,288]{1,2,0:T(8,128)(2,1)S(1)}, u32[]{:S(2)}, u32[]{:S(2)}) %all-to-all-start) | async-done | bytes 294944 | tf_op jit(solution)/shard_map/all_to_all | solution.py:177
  229.0 2.3 copy-done.5
  234.1 3.7 %all-to-all-start.1 = ((bf16[1,2,64,1152]{3,1,0,2:T(2,128)(2,1)}), bf16[1,2,64,1152]{3,1,0,2:T(2,128)(2,1)S(1)}, u32[]{:S(2)}, u32[]{:S(2)}) async-start(bf16[1,2,64,1152]{3,1,0,2:T(2,128)(2,1)} %copy.101), calls=%async_computation.1 | async-start | bytes 589824 | tf_op jit(solution)/shard_map/all_to_all | solution.py:182
  237.9 6.0 %all-to-all-done.1 = bf16[1,2,64,1152]{3,1,0,2:T(2,128)(2,1)S(1)} async-done(((bf16[1,2,64,1152]{3,1,0,2:T(2,128)(2,1)}), bf16[1,2,64,1152]{3,1,0,2:T(2,128)(2,1)S(1)}, u32[]{:S(2)}, u32[]{:S(2)}) %all-to-all-start.1) | async-done | bytes 294944 | tf_op jit(solution)/shard_map/all_to_all | solution.py:182
  245.3 4.0 %copy-done.2 = bf16[1,1152,4608]{2,1,0:T(8,128)(2,1)S(1)} copy-done((bf16[1,1152,4608]{2,1,0:T(8,128)(2,1)S(1)}, bf16[1,1152,4608]{2,1,0:T(8,128)(2,1)}, u32[]{:S(2)}) %copy-start.2) | copy-done | bytes 10616856
  249.3 3.9 %shard_map.150 = f32[128,3456]{1,0:T(8,128)S(1)} custom-call(bf16[128,1152]{1,0:T(8,128)(2,1)S(1)} %fusion.19.x_ref, bf16[1152,4608]{1,0:T(8,128)(2,1)S(1)} %bitcast.182), custom_call_target="tpu_custom_call" | custom-call | flops 1019215872 | bytes 10027008 | tf_op jit(solution)/shard_map/pallas_call | solution.py:67
  256.3 4.0 %copy-done.3 = bf16[1,1152,4608]{2,1,0:T(8,128)(2,1)S(1)} copy-done((bf16[1,1152,4608]{2,1,0:T(8,128)(2,1)S(1)}, bf16[1,1152,4608]{2,1,0:T(8,128)(2,1)}, u32[]{:S(2)}) %copy-start.3) | copy-done | bytes 10616856
  (202 shorter events, 71.9 us)
Async XLA Ops:
  6.5 110.4 %all-gather.7.cloned.1.call-start = ((), (), s32[]{:S(2)}) async-start(), calls=%async_computation.2 | async-start | bytes 8957952 | tf_op jit(solution)/shard_map/all_gather | solution.py:35
  9.1 172.7 %all-gather.9.cloned.1.call-start = ((), (), s32[]{:S(2)}) async-start(), calls=%async_computation.3 | async-start | bytes 5308416 | tf_op jit(solution)/shard_map/all_gather | solution.py:35
  19.9 224.8 %all-gather.11.cloned.1.call-start = ((), (), s32[]{:S(2)}) async-start(), calls=%async_computation.4 | async-start | bytes 11943936 | tf_op jit(solution)/shard_map/all_gather | solution.py:35
  20.2 5.9 %copy-start.18 = (bf16[288,1152]{1,0:T(8,128)(2,1)S(1)}, bf16[288,1152]{1,0:T(8,128)(2,1)}, u32[]{:S(2)}) copy-start(bf16[288,1152]{1,0:T(8,128)(2,1)} %param.21) | copy-start | bytes 1990660
  20.2 6.2 %copy-start.8 = (bf16[1,2,64,1152]{3,2,1,0:T(8,128)(2,1)S(1)}, bf16[1,2,64,1152]{3,2,1,0:T(8,128)(2,1)}, u32[]{:S(2)}) copy-start(bf16[1,2,64,1152]{3,2,1,0:T(8,128)(2,1)} %param.15) | copy-start | bytes 884740
  20.2 6.2 %copy-start.13 = (bf16[1,2,64,1152]{3,2,1,0:T(8,128)(2,1)S(1)}, bf16[1,2,64,1152]{3,2,1,0:T(8,128)(2,1)}, u32[]{:S(2)}) copy-start(bf16[1,2,64,1152]{3,2,1,0:T(8,128)(2,1)} %param.16) | copy-start | bytes 884740
  20.2 7.9 %copy-start.26 = (f32[3,1152]{1,0:T(4,128)S(1)}, f32[3,1152]{1,0:T(4,128)}, u32[]{:S(2)}) copy-start(f32[3,1152]{1,0:T(4,128)} %param.26) | copy-start | bytes 41476
  20.2 8.5 %copy-start.27 = (f32[3,1152]{1,0:T(4,128)S(1)}, f32[3,1152]{1,0:T(4,128)}, u32[]{:S(2)}) copy-start(f32[3,1152]{1,0:T(4,128)} %param.27) | copy-start | bytes 41476
  20.2 9.2 %copy-start.29 = (f32[3,2,72]{2,1,0:T(2,128)S(1)}, f32[3,2,72]{2,1,0:T(2,128)}, u32[]{:S(2)}) copy-start(f32[3,2,72]{2,1,0:T(2,128)} %param.29) | copy-start | bytes 5188
  21.5 25.5 %collective-permute-start = (bf16[288,1152]{1,0:T(8,128)(2,1)S(1)}, bf16[288,1152]{1,0:T(8,128)(2,1)S(1)}, u32[]{:S(2)}, u32[]{:S(2)}) collective-permute-start(bf16[288,1152]{1,0:T(8,128)(2,1)S(1)} %copy-done.17), channel_id=1, source_target_pairs={{0,8},{8,16},{16,24},{24,0},{1,9},{9,17},{17,25},{25,1},{2,10},{10... | collective-permute-start | bytes 1990664 | tf_op jit(solution)/shard_map/ppermute | solution.py:41
  22.0 25.7 %collective-permute-start.1 = (bf16[288,1152]{1,0:T(8,128)(2,1)S(1)}, bf16[288,1152]{1,0:T(8,128)(2,1)}, u32[]{:S(2)}, u32[]{:S(2)}) collective-permute-start(bf16[288,1152]{1,0:T(8,128)(2,1)S(1)} %copy-done.17), channel_id=1, source_target_pairs={{0,16},{8,24},{16,0},{24,8},{1,17},{9,25},{17,1},{25,9},{2,18},{10... | collective-permute-start | bytes 1990664 | tf_op jit(solution)/shard_map/ppermute | solution.py:41
  24.7 49.0 %collective-permute-start.2 = (bf16[288,1152]{1,0:T(8,128)(2,1)S(1)}, bf16[288,1152]{1,0:T(8,128)(2,1)}, u32[]{:S(2)}, u32[]{:S(2)}) collective-permute-start(bf16[288,1152]{1,0:T(8,128)(2,1)S(1)} %copy-done.17), channel_id=1, source_target_pairs={{0,24},{8,0},{16,8},{24,16},{1,25},{9,1},{17,9},{25,17},{2,26},{10... | collective-permute-start | bytes 1990664 | tf_op jit(solution)/shard_map/ppermute | solution.py:41
  26.0 70.7 %collective-permute-start.3 = (bf16[288,1152]{1,0:T(8,128)(2,1)S(1)}, bf16[288,1152]{1,0:T(8,128)(2,1)S(1)}, u32[]{:S(2)}, u32[]{:S(2)}) collective-permute-start(bf16[288,1152]{1,0:T(8,128)(2,1)S(1)} %copy-done.18), channel_id=1, source_target_pairs={{0,8},{8,16},{16,24},{24,0},{1,9},{9,17},{17,25},{25,1},{2,10},{10... | collective-permute-start | bytes 1990664 | tf_op jit(solution)/shard_map/ppermute | solution.py:41
  26.0 71.4 %collective-permute-start.4 = (bf16[288,1152]{1,0:T(8,128)(2,1)S(1)}, bf16[288,1152]{1,0:T(8,128)(2,1)}, u32[]{:S(2)}, u32[]{:S(2)}) collective-permute-start(bf16[288,1152]{1,0:T(8,128)(2,1)S(1)} %copy-done.18), channel_id=1, source_target_pairs={{0,16},{8,24},{16,0},{24,8},{1,17},{9,25},{17,1},{25,9},{2,18},{10... | collective-permute-start | bytes 1990664 | tf_op jit(solution)/shard_map/ppermute | solution.py:41
  30.2 85.3 %copy-start.19 = (bf16[288,1152]{1,0:T(8,128)(2,1)S(1)}, bf16[288,1152]{1,0:T(8,128)(2,1)}, u32[]{:S(2)}) copy-start(bf16[288,1152]{1,0:T(8,128)(2,1)} %param.21) | copy-start | bytes 1990660
  47.0 68.5 %collective-permute-start.5 = (bf16[288,1152]{1,0:T(8,128)(2,1)S(1)}, bf16[288,1152]{1,0:T(8,128)(2,1)S(1)}, u32[]{:S(2)}, u32[]{:S(2)}) collective-permute-start(bf16[288,1152]{1,0:T(8,128)(2,1)S(1)} %copy-done.18), channel_id=1, source_target_pairs={{0,24},{8,0},{16,8},{24,16},{1,25},{9,1},{17,9},{25,17},{2,26},{10... | collective-permute-start | bytes 1990664 | tf_op jit(solution)/shard_map/ppermute | solution.py:41
  117.0 3.3 %copy-start.6 = (bf16[1,1152,3456]{2,1,0:T(8,128)(2,1)S(1)}, bf16[1,1152,3456]{2,1,0:T(8,128)(2,1)}, u32[]{:S(2)}) copy-start(bf16[1,1152,3456]{2,1,0:T(8,128)(2,1)} %all-gather.7.cloned.1.call-done) | copy-start | bytes 23887876
  154.5 4.3 %copy-start.24 = (f32[1152]{0:T(1024)S(1)}, f32[1152]{0:T(1024)}, u32[]{:S(2)}) copy-start(f32[1152]{0:T(1024)} %get-tuple-element.17) | copy-start | bytes 13828
  163.1 6.5 %copy-start.33 = (s32[4]{0:T(128)S(1)}, s32[4]{0:T(128)}, u32[]{:S(2)}) copy-start(s32[4]{0:T(128)} %param.17) | copy-start | bytes 52
  163.1 17.4 %copy-start.30 = (s32[4]{0:T(128)S(1)}, s32[4]{0:T(128)}, u32[]{:S(2)}) copy-start(s32[4]{0:T(128)} %get-tuple-element.39) | copy-start | bytes 52
  163.7 10.6 %collective-permute-start.7 = (bf16[128,1152]{1,0:T(8,128)(2,1)S(1)}, bf16[128,1152]{1,0:T(8,128)(2,1)S(1)}, u32[]{:S(2)}, u32[]{:S(2)}) collective-permute-start(bf16[128,1152]{1,0:T(8,128)(2,1)S(1)} %add_convert_fusion.1), channel_id=1, source_target_pairs={{2,0},{4,2},{6,4},{3,1},{5,3},{7,5},{10,8},{12,10},{14,12},{11,9},... | collective-permute-start | bytes 884744 | tf_op jit(solution)/shard_map/ppermute | solution.py:161
  165.0 11.1 %collective-permute-start.6 = (bf16[128,1152]{1,0:T(8,128)(2,1)S(1)}, bf16[128,1152]{1,0:T(8,128)(2,1)S(1)}, u32[]{:S(2)}, u32[]{:S(2)}) collective-permute-start(bf16[128,1152]{1,0:T(8,128)(2,1)S(1)} %add_convert_fusion.1), channel_id=1, source_target_pairs={{0,2},{2,4},{4,6},{1,3},{3,5},{5,7},{8,10},{10,12},{12,14},{9,11},... | collective-permute-start | bytes 884744 | tf_op jit(solution)/shard_map/ppermute | solution.py:160
  174.2 11.5 %collective-permute-start.8 = (bf16[128,1152]{1,0:T(8,128)(2,1)S(1)}, bf16[128,1152]{1,0:T(8,128)(2,1)S(1)}, u32[]{:S(2)}, u32[]{:S(2)}) collective-permute-start(bf16[128,1152]{1,0:T(8,128)(2,1)S(1)} %collective-permute-done.7), channel_id=1, source_target_pairs={{2,0},{4,2},{6,4},{3,1},{5,3},{7,5},{10,8},{12,10},{14,12},{11,9},... | collective-permute-start | bytes 884744 | tf_op jit(solution)/shard_map/ppermute | solution.py:161
  176.0 11.6 %collective-permute-start.10 = (bf16[128,1152]{1,0:T(8,128)(2,1)S(1)}, bf16[128,1152]{1,0:T(8,128)(2,1)S(1)}, u32[]{:S(2)}, u32[]{:S(2)}) collective-permute-start(bf16[128,1152]{1,0:T(8,128)(2,1)S(1)} %collective-permute-done.6), channel_id=1, source_target_pairs={{0,2},{2,4},{4,6},{1,3},{3,5},{5,7},{8,10},{10,12},{12,14},{9,11},... | collective-permute-start | bytes 884744 | tf_op jit(solution)/shard_map/ppermute | solution.py:160
  185.7 11.7 %collective-permute-start.9 = (bf16[128,1152]{1,0:T(8,128)(2,1)S(1)}, bf16[128,1152]{1,0:T(8,128)(2,1)S(1)}, u32[]{:S(2)}, u32[]{:S(2)}) collective-permute-start(bf16[128,1152]{1,0:T(8,128)(2,1)S(1)} %collective-permute-done.8), channel_id=1, source_target_pairs={{2,0},{4,2},{6,4},{3,1},{5,3},{7,5},{10,8},{12,10},{14,12},{11,9},... | collective-permute-start | bytes 884744 | tf_op jit(solution)/shard_map/ppermute | solution.py:161
  187.7 11.1 %collective-permute-start.11 = (bf16[128,1152]{1,0:T(8,128)(2,1)S(1)}, bf16[128,1152]{1,0:T(8,128)(2,1)S(1)}, u32[]{:S(2)}, u32[]{:S(2)}) collective-permute-start(bf16[128,1152]{1,0:T(8,128)(2,1)S(1)} %collective-permute-done.10), channel_id=1, source_target_pairs={{0,2},{2,4},{4,6},{1,3},{3,5},{5,7},{8,10},{10,12},{12,14},{9,11},... | collective-permute-start | bytes 884744 | tf_op jit(solution)/shard_map/ppermute | solution.py:160
  211.4 8.2 %copy-start.34 = (s32[4]{0:T(128)S(1)}, s32[4]{0:T(128)}, u32[]{:S(2)}) copy-start(s32[4]{0:T(128)} %param.18) | copy-start | bytes 52
  211.4 9.3 %copy-start.28 = (f32[3,1152]{1,0:T(4,128)S(1)}, f32[3,1152]{1,0:T(4,128)}, u32[]{:S(2)}) copy-start(f32[3,1152]{1,0:T(4,128)} %param.28) | copy-start | bytes 41476
  213.7 15.1 %all-to-all-start = ((bf16[4,128,288]{1,2,0:T(8,128)(2,1)}), bf16[4,128,288]{1,2,0:T(8,128)(2,1)S(1)}, u32[]{:S(2)}, u32[]{:S(2)}) async-start(bf16[4,128,288]{1,2,0:T(8,128)(2,1)} %gather_fusion.4), calls=%async_computation | async-start | bytes 589824 | tf_op jit(solution)/shard_map/all_to_all | solution.py:177
  234.1 9.8 %all-to-all-start.1 = ((bf16[1,2,64,1152]{3,1,0,2:T(2,128)(2,1)}), bf16[1,2,64,1152]{3,1,0,2:T(2,128)(2,1)S(1)}, u32[]{:S(2)}, u32[]{:S(2)}) async-start(bf16[1,2,64,1152]{3,1,0,2:T(2,128)(2,1)} %copy.101), calls=%async_computation.1 | async-start | bytes 589824 | tf_op jit(solution)/shard_map/all_to_all | solution.py:182
  245.3 4.0 %copy-start.2 = (bf16[1,1152,4608]{2,1,0:T(8,128)(2,1)S(1)}, bf16[1,1152,4608]{2,1,0:T(8,128)(2,1)}, u32[]{:S(2)}) copy-start(bf16[1,1152,4608]{2,1,0:T(8,128)(2,1)} %all-gather.11.cloned.1.call-done) | copy-start | bytes 31850500
  256.3 4.0 %copy-start.3 = (bf16[1,1152,4608]{2,1,0:T(8,128)(2,1)S(1)}, bf16[1,1152,4608]{2,1,0:T(8,128)(2,1)}, u32[]{:S(2)}) copy-start(bf16[1,1152,4608]{2,1,0:T(8,128)(2,1)} %all-gather.11.cloned.1.call-done) | copy-start | bytes 31850500
  (20 other events, 32.6 us)
Sparse Core Ops, SparseCore 0:
  9.3 82.5 all-gather.6
  93.8 45.0 all-gather.8
  140.8 63.8 all-gather.10

commit v2 on v1

--- a/solution.py
+++ b/solution.py
@@ -33,20 +33,6 @@
     shares = weight.reshape(dp_size, rows // dp_size, columns)
     own_share = lax.dynamic_index_in_dim(shares, lax.axis_index("dp"), 0, keepdims=False)
     return lax.all_gather(own_share, ("seq", "dp"), axis=0, tiled=True)
-
-
-def pass_rows(weight, seq_size):
-    pieces = [weight]
-    for k in range(1, seq_size):
-        pieces.append(lax.ppermute(weight, "seq", [(i, (i + k) % seq_size) for i in range(seq_size)]))
-    order = (lax.axis_index("seq") - jnp.arange(seq_size)) % seq_size
-    return jnp.concatenate(pieces, axis=0), order
-
-
-def project_passed(inputs, passed):
-    weight, order = passed
-    chunks = inputs.reshape(inputs.shape[0], order.shape[0], -1)
-    return project(jnp.take(chunks, order, axis=1, mode="clip").reshape(inputs.shape), weight)
 
 
 def tile_of(size, unit, largest):
@@ -110,7 +96,6 @@
 
 
 def per_device(
-    seq_size,
     view_size,
     dp_size,
     latent,
@@ -136,9 +121,8 @@
     view_heads = HEADS // view_size
     collect = lambda weight: collect_rows(weight, dp_size)
 
-    out_ctrl = pass_rows(w_out_ctrl, seq_size)
-    join = pass_rows(w_join, seq_size)
     qkv_ctrl = collect(w_qkv_ctrl)
+    ctrl = collect(jnp.concatenate([w_out_ctrl, w_join], axis=1))
     columns = w_qkv_space.reshape(-1, 3, view_size, width // view_size)
     columns = lax.dynamic_index_in_dim(columns, view, 2, keepdims=False)
     space = collect(jnp.concatenate([w_out_space, columns.reshape(-1, 3 * width // view_size)], axis=1))
@@ -151,8 +135,8 @@
     by_frame = [part.reshape(HEADS * frames_here, patches, head_size) for part in parts]
     attended = attend(*by_frame, None).reshape(HEADS, tokens, head_size)
     flat = attended.transpose(1, 0, 2).reshape(tokens, width)
-    control = (ctrl_in + mod_ctrl[2] * project_passed(flat, out_ctrl)).astype(jnp.bfloat16)
-    joined = base + project_passed(control, join)
+    control = (ctrl_in + mod_ctrl[2] * project(flat, ctrl, 0, width)).astype(jnp.bfloat16)
+    joined = base + project(control, ctrl, width, width)
 
     normed = modulate(joined, mod_space)
     upward, downward = [normed], [normed]
@@ -212,7 +196,7 @@
         P("dp", None),
         P(),
     )
-    sizes = mesh.shape["seq"], mesh.shape["view"], mesh.shape["dp"]
+    sizes = mesh.shape["view"], mesh.shape["dp"]
 
     def run(*arrays):
         return per_device(*sizes, *arrays)

time: 270 us -> 245 us (0.907)
  other arithmetic: 26.5 us -> 15.6 us
  local copies, waits for them, and re-layouts: 67.6 us -> 58.6 us
  starting transfers between devices: 32.1 us -> 27.4 us
    all_gather x3 -> x4, waiting for transfers between devices: 0.04 us -> 80.3 us  [collect_rows(): return lax.all_gather(own_share, ('seq', 'dp'), axis=0, tiled=True)]
    ppermute x6 -> x0, waiting for transfers between devices: 80.2 us -> none  [pass_rows(): lax.ppermute(weight, 'seq', [(i, (i + k) % seq_size) for i in range(seq_s...]
    concatenate x2 -> x1, other arithmetic: 6.43 us -> 0.1 us  [per_device(): ctrl = collect(jnp.concatenate([w_out_ctrl, w_join], axis=1))]
    ppermute x6 -> x0, starting transfers between devices: 4.98 us -> none  [pass_rows(): lax.ppermute(weight, 'seq', [(i, (i + k) % seq_size) for i in range(seq_s...]
    all_to_all x1, waiting for transfers between devices: 5.99 us -> 9.47 us  [per_device(): lax.all_to_all(spaced, 'seq', split_axis=2, concat_axis=1, tiled=True)]
    unnamed x70 -> x42, local copies, waits for them, and re-layouts: 19.9 us -> 20 us
  transfers between devices with their start and end apart: 17 -> 12, of which waited for: 14 -> 9; matrix products, arithmetic and copies ran while one was open for 28% -> 21% of each run, Pallas kernels for 4% -> 4%
where the time goes in v2:
time: 245 us; the launch traced here: 244 us
  waiting for transfers between devices  108 us (44%)
  local copies, waits for them, and re-layouts  58.6 us (24%)
  starting transfers between devices  27.4 us (11%)
  other arithmetic  15.6 us (6%)
  Pallas kernels  14.9 us (6%)
  between operations  13.8 us (6%)
  matrix products  5.45 us (2%)
    all_gather x4, waiting for transfers between devices, collect_rows(): return lax.all_gather(own_share, ('seq', 'dp'), axis=0, tiled=True)  80.3 us
    unnamed x42, local copies, waits for them, and re-layouts  20 us
    pallas_call x7, Pallas kernels, project(): pl.pallas_call(matmul_kernel, grid=(rows // row_tile, columns // column_t...  14.9 us
    ppermute x3, starting transfers between devices, per_device(): lax.ppermute(upward[-1], 'view', [(i, i + 1) for i in range(view_size - 1)])  13.9 us
    ppermute x3, waiting for transfers between devices, per_device(): lax.ppermute(downward[-1], 'view', [(i + 1, i) for i in range(view_size -...  9.75 us
    all_to_all x1, waiting for transfers between devices, per_device(): lax.all_to_all(spaced, 'seq', split_axis=2, concat_axis=1, tiled=True)  9.47 us
    all_to_all x1, waiting for transfers between devices, per_device(): lax.all_to_all(attended[cameras], 'view', split_axis=0, concat_axis=0, ti...  7.62 us
    dynamic_slice x1, local copies, waits for them, and re-layouts, per_device(): columns = lax.dynamic_index_in_dim(columns, view, 2, keepdims=False)  6.32 us
  transfers between devices with their start and end apart: 12, of which 9 were waited for; matrix products, arithmetic and copies ran while one was open for 21% of the time, Pallas kernels for 4%

profile of v2, /device:TPU:0, one launch (start us, length us, event | category | flops | bytes accessed | tf_op | source)
XLA Modules:
  0.0 244.1 jit_solution(11093452584969708358)
XLA Ops:
  6.6 1.5 copy-done
  10.3 4.7 %reshape.446 = bf16[288,3,4,288]{3,2,1,0:T(4,128)(2,1)} reshape(bf16[288,3456]{1,0:T(8,128)(2,1)} %param.22) | data formatting | bytes 3981312 | tf_op jit(solution)/shard_map/reshape | solution.py:126
  15.0 6.3 %dynamic-slice_reduce_fusion = bf16[288,3,288]{2,1,0:T(4,128)(2,1)S(1)} fusion(bf16[288,3,4,288]{3,2,1,0:T(4,128)(2,1)} %reshape.446, s32[]{:T(128)S(6)} %select_n.109), kind=kLoop, calls=%fused_computation.14 | loop fusion | bytes 995332 | tf_op jit(solution)/shard_map/jit(dynamic_index_in_dim)/dynamic_slice | solution.py:127
  23.0 1.7 pad_maximum_fusion
  27.0 37.5 %all-gather.9.cloned.1.call-done = bf16[1,1152,3456]{2,1,0:T(8,128)(2,1)} async-done(((bf16[1,144,3456]{2,1,0:T(8,128)(2,1)}), bf16[1,1152,3456]{2,1,0:T(8,128)(2,1)}) %all-gather.9.cloned.1.call-update) | async-done | bytes 7962640 | tf_op jit(solution)/shard_map/all_gather | solution.py:35
  64.6 3.3 %copy-done.7 = bf16[1,1152,3456]{2,1,0:T(8,128)(2,1)S(1)} copy-done((bf16[1,1152,3456]{2,1,0:T(8,128)(2,1)S(1)}, bf16[1,1152,3456]{2,1,0:T(8,128)(2,1)}, u32[]{:S(2)}) %copy-start.7) | copy-done | bytes 7962648
  67.8 3.9 %shard_map.145 = f32[128,3456]{1,0:T(8,128)S(1)} custom-call(bf16[128,1152]{1,0:T(8,128)(2,1)S(1)} %add_convert_fusion.3.x_ref, bf16[1152,3456]{1,0:T(8,128)(2,1)S(1)} %bitcast.181), custom_call_target="tpu_custom_call" | custom-call | flops 1019215872 | bytes 10027008 | tf_op jit(solution)/shard_map/pallas_call | solution.py:53
  71.8 1.7 copy.77
  78.4 1.6 multiply_convert_fusion.2
  81.8 26.1 %all-gather.11.cloned.1.call-done = bf16[1,1152,2304]{2,1,0:T(8,128)(2,1)} async-done(((bf16[1,144,2304]{2,1,0:T(8,128)(2,1)}), bf16[1,1152,2304]{2,1,0:T(8,128)(2,1)}) %all-gather.11.cloned.1.call-update) | async-done | bytes 5308432 | tf_op jit(solution)/shard_map/all_gather | solution.py:35
  107.9 2.5 %copy-done.4 = bf16[1,1152,2304]{2,1,0:T(8,128)(2,1)S(1)} copy-done((bf16[1,1152,2304]{2,1,0:T(8,128)(2,1)S(1)}, bf16[1,1152,2304]{2,1,0:T(8,128)(2,1)}, u32[]{:S(2)}) %copy-start.4) | copy-done | bytes 5308440
  116.1 4.6 %collective-permute-start = (bf16[128,1152]{1,0:T(8,128)(2,1)S(1)}, bf16[128,1152]{1,0:T(8,128)(2,1)S(1)}, u32[]{:S(2)}, u32[]{:S(2)}) collective-permute-start(bf16[128,1152]{1,0:T(8,128)(2,1)S(1)} %add_convert_fusion.1), channel_id=1, source_target_pairs={{0,2},{2,4},{4,6},{1,3},{3,5},{5,7},{8,10},{10,12},{12,14},{9,11},... | collective-permute-start | bytes 884744 | tf_op jit(solution)/shard_map/ppermute | solution.py:144
  121.1 4.8 %collective-permute-done.1 = bf16[128,1152]{1,0:T(8,128)(2,1)S(1)} collective-permute-done((bf16[128,1152]{1,0:T(8,128)(2,1)S(1)}, bf16[128,1152]{1,0:T(8,128)(2,1)S(1)}, u32[]{:S(2)}, u32[]{:S(2)}) %collective-permute-start.1) | collective-permute-done | bytes 294944 | tf_op jit(solution)/shard_map/ppermute | solution.py:145
  127.2 4.6 %collective-permute-start.4 = (bf16[128,1152]{1,0:T(8,128)(2,1)S(1)}, bf16[128,1152]{1,0:T(8,128)(2,1)S(1)}, u32[]{:S(2)}, u32[]{:S(2)}) collective-permute-start(bf16[128,1152]{1,0:T(8,128)(2,1)S(1)} %collective-permute-done), channel_id=1, source_target_pairs={{0,2},{2,4},{4,6},{1,3},{3,5},{5,7},{8,10},{10,12},{12,14},{9,11},... | collective-permute-start | bytes 884744 | tf_op jit(solution)/shard_map/ppermute | solution.py:144
  133.2 15.5 %all-gather.13.cloned.1.call-done = bf16[1,1152,2016]{2,1,0:T(8,128)(2,1)} async-done(((bf16[1,144,2016]{2,1,0:T(8,128)(2,1)}), bf16[1,1152,2016]{2,1,0:T(8,128)(2,1)}) %all-gather.13.cloned.1.call-update) | async-done | bytes 4644880 | tf_op jit(solution)/shard_map/all_gather | solution.py:35
  148.7 1.7 slice.137.w_ref
  151.8 4.8 %collective-permute-start.5 = (bf16[128,1152]{1,0:T(8,128)(2,1)S(1)}, bf16[128,1152]{1,0:T(8,128)(2,1)S(1)}, u32[]{:S(2)}, u32[]{:S(2)}) collective-permute-start(bf16[128,1152]{1,0:T(8,128)(2,1)S(1)} %collective-permute-done.4), channel_id=1, source_target_pairs={{0,2},{2,4},{4,6},{1,3},{3,5},{5,7},{8,10},{10,12},{12,14},{9,11},... | collective-permute-start | bytes 884744 | tf_op jit(solution)/shard_map/ppermute | solution.py:144
  156.6 4.9 %collective-permute-done.3 = bf16[128,1152]{1,0:T(8,128)(2,1)S(1)} collective-permute-done((bf16[128,1152]{1,0:T(8,128)(2,1)S(1)}, bf16[128,1152]{1,0:T(8,128)(2,1)S(1)}, u32[]{:S(2)}, u32[]{:S(2)}) %collective-permute-start.3) | collective-permute-done | bytes 294944 | tf_op jit(solution)/shard_map/ppermute | solution.py:145
  165.7 2.8 %copy.89 = f32[512,864]{0,1:T(8,128)} copy(f32[512,864]{1,0:T(8,128)} %copy-done.8) | data formatting | bytes 3538944 | tf_op jit(solution)/shard_map/pallas_call | solution.py:53
  169.6 2.2 multiply_reduce_fusion.3
  171.8 1.9 squeeze.55
  181.8 5.6 %all-to-all-start = ((bf16[4,128,288]{1,2,0:T(8,128)(2,1)}), bf16[4,128,288]{1,2,0:T(8,128)(2,1)S(1)}, u32[]{:S(2)}, u32[]{:S(2)}) async-start(bf16[4,128,288]{1,2,0:T(8,128)(2,1)} %gather_fusion.2), calls=%async_computation | async-start | bytes 589824 | tf_op jit(solution)/shard_map/all_to_all | solution.py:161
  188.7 7.6 %all-to-all-done = bf16[4,128,288]{1,2,0:T(8,128)(2,1)S(1)} async-done(((bf16[4,128,288]{1,2,0:T(8,128)(2,1)}), bf16[4,128,288]{1,2,0:T(8,128)(2,1)S(1)}, u32[]{:S(2)}, u32[]{:S(2)}) %all-to-all-start) | async-done | bytes 294944 | tf_op jit(solution)/shard_map/all_to_all | solution.py:161
  196.6 2.3 copy-done.6
  198.9 1.6 shard_map.149
  201.6 3.7 %all-to-all-start.1 = ((bf16[1,2,64,1152]{3,1,0,2:T(2,128)(2,1)}), bf16[1,2,64,1152]{3,1,0,2:T(2,128)(2,1)S(1)}, u32[]{:S(2)}, u32[]{:S(2)}) async-start(bf16[1,2,64,1152]{3,1,0,2:T(2,128)(2,1)} %copy.96), calls=%async_computation.1 | async-start | bytes 589824 | tf_op jit(solution)/shard_map/all_to_all | solution.py:166
  205.5 9.5 %all-to-all-done.1 = bf16[1,2,64,1152]{3,1,0,2:T(2,128)(2,1)S(1)} async-done(((bf16[1,2,64,1152]{3,1,0,2:T(2,128)(2,1)}), bf16[1,2,64,1152]{3,1,0,2:T(2,128)(2,1)S(1)}, u32[]{:S(2)}, u32[]{:S(2)}) %all-to-all-start.1) | async-done | bytes 294944 | tf_op jit(solution)/shard_map/all_to_all | solution.py:166
  217.0 4.0 %copy-done.2 = bf16[1,1152,4608]{2,1,0:T(8,128)(2,1)S(1)} copy-done((bf16[1,1152,4608]{2,1,0:T(8,128)(2,1)S(1)}, bf16[1,1152,4608]{2,1,0:T(8,128)(2,1)}, u32[]{:S(2)}) %copy-start.2) | copy-done | bytes 10616856
  221.0 3.9 %shard_map.150 = f32[128,3456]{1,0:T(8,128)S(1)} custom-call(bf16[128,1152]{1,0:T(8,128)(2,1)S(1)} %fusion.19.x_ref, bf16[1152,4608]{1,0:T(8,128)(2,1)S(1)} %bitcast.175), custom_call_target="tpu_custom_call" | custom-call | flops 1019215872 | bytes 10027008 | tf_op jit(solution)/shard_map/pallas_call | solution.py:53
  224.9 1.7 copy.101
  228.0 1.7 fusion.56
  231.5 4.0 %copy-done.3 = bf16[1,1152,4608]{2,1,0:T(8,128)(2,1)S(1)} copy-done((bf16[1,1152,4608]{2,1,0:T(8,128)(2,1)S(1)}, bf16[1,1152,4608]{2,1,0:T(8,128)(2,1)}, u32[]{:S(2)}) %copy-start.3) | copy-done | bytes 10616856
  (160 shorter events, 46.0 us)
Async XLA Ops:
  6.5 1.6 copy-start
  6.5 2.6 %copy-start.12 = (bf16[288,1152]{1,0:T(8,128)(2,1)S(1)}, bf16[288,1152]{1,0:T(8,128)(2,1)}, u32[]{:S(2)}) copy-start(bf16[288,1152]{1,0:T(8,128)(2,1)} %param.20) | copy-start | bytes 1990660
  6.5 2.7 %copy-start.11 = (bf16[288,1152]{1,0:T(8,128)(2,1)S(1)}, bf16[288,1152]{1,0:T(8,128)(2,1)}, u32[]{:S(2)}) copy-start(bf16[288,1152]{1,0:T(8,128)(2,1)} %param.21) | copy-start | bytes 1990660
  6.5 58.0 %all-gather.9.cloned.1.call-start = ((), (), s32[]{:S(2)}) async-start(), calls=%async_computation.2 | async-start | bytes 8957952 | tf_op jit(solution)/shard_map/all_gather | solution.py:35
  9.1 98.7 %all-gather.11.cloned.1.call-start = ((), (), s32[]{:S(2)}) async-start(), calls=%async_computation.3 | async-start | bytes 5971968 | tf_op jit(solution)/shard_map/all_gather | solution.py:35
  10.2 138.5 %all-gather.13.cloned.1.call-start = ((), (), s32[]{:S(2)}) async-start(), calls=%async_computation.4 | async-start | bytes 5308416 | tf_op jit(solution)/shard_map/all_gather | solution.py:35
  15.0 6.9 %copy-start.13 = (bf16[288,1152]{1,0:T(8,128)(2,1)S(1)}, bf16[288,1152]{1,0:T(8,128)(2,1)}, u32[]{:S(2)}) copy-start(bf16[288,1152]{1,0:T(8,128)(2,1)} %param.23) | copy-start | bytes 1990660
  21.3 1.8 copy-start.14
  22.8 194.2 %all-gather.15.cloned.1.call-start = ((), (), s32[]{:S(2)}) async-start(), calls=%async_computation.5 | async-start | bytes 11943936 | tf_op jit(solution)/shard_map/all_gather | solution.py:35
  24.8 1.3 copy-start.19
  24.8 1.3 copy-start.9
  24.8 1.3 copy-start.10
  26.0 0.8 copy-start.16
  26.0 0.8 copy-start.18
  64.6 3.3 %copy-start.7 = (bf16[1,1152,3456]{2,1,0:T(8,128)(2,1)S(1)}, bf16[1,1152,3456]{2,1,0:T(8,128)(2,1)}, u32[]{:S(2)}) copy-start(bf16[1,1152,3456]{2,1,0:T(8,128)(2,1)} %all-gather.9.cloned.1.call-done) | copy-start | bytes 23887876
  107.9 2.5 %copy-start.4 = (bf16[1,1152,2304]{2,1,0:T(8,128)(2,1)S(1)}, bf16[1,1152,2304]{2,1,0:T(8,128)(2,1)}, u32[]{:S(2)}) copy-start(bf16[1,1152,2304]{2,1,0:T(8,128)(2,1)} %all-gather.11.cloned.1.call-done) | copy-start | bytes 15925252
  110.4 2.5 %copy-start.5 = (bf16[1,1152,2304]{2,1,0:T(8,128)(2,1)S(1)}, bf16[1,1152,2304]{2,1,0:T(8,128)(2,1)}, u32[]{:S(2)}) copy-start(bf16[1,1152,2304]{2,1,0:T(8,128)(2,1)} %all-gather.11.cloned.1.call-done) | copy-start | bytes 15925252
  114.8 11.1 %collective-permute-start.1 = (bf16[128,1152]{1,0:T(8,128)(2,1)S(1)}, bf16[128,1152]{1,0:T(8,128)(2,1)S(1)}, u32[]{:S(2)}, u32[]{:S(2)}) collective-permute-start(bf16[128,1152]{1,0:T(8,128)(2,1)S(1)} %add_convert_fusion.1), channel_id=1, source_target_pairs={{2,0},{4,2},{6,4},{3,1},{5,3},{7,5},{10,8},{12,10},{14,12},{11,9},... | collective-permute-start | bytes 884744 | tf_op jit(solution)/shard_map/ppermute | solution.py:145
  116.1 11.1 %collective-permute-start = (bf16[128,1152]{1,0:T(8,128)(2,1)S(1)}, bf16[128,1152]{1,0:T(8,128)(2,1)S(1)}, u32[]{:S(2)}, u32[]{:S(2)}) collective-permute-start(bf16[128,1152]{1,0:T(8,128)(2,1)S(1)} %add_convert_fusion.1), channel_id=1, source_target_pairs={{0,2},{2,4},{4,6},{1,3},{3,5},{5,7},{8,10},{10,12},{12,14},{9,11},... | collective-permute-start | bytes 884744 | tf_op jit(solution)/shard_map/ppermute | solution.py:144
  125.9 24.6 %collective-permute-start.2 = (bf16[128,1152]{1,0:T(8,128)(2,1)S(1)}, bf16[128,1152]{1,0:T(8,128)(2,1)S(1)}, u32[]{:S(2)}, u32[]{:S(2)}) collective-permute-start(bf16[128,1152]{1,0:T(8,128)(2,1)S(1)} %collective-permute-done.1), channel_id=1, source_target_pairs={{2,0},{4,2},{6,4},{3,1},{5,3},{7,5},{10,8},{12,10},{14,12},{11,9},... | collective-permute-start | bytes 884744 | tf_op jit(solution)/shard_map/ppermute | solution.py:145
  127.2 24.6 %collective-permute-start.4 = (bf16[128,1152]{1,0:T(8,128)(2,1)S(1)}, bf16[128,1152]{1,0:T(8,128)(2,1)S(1)}, u32[]{:S(2)}, u32[]{:S(2)}) collective-permute-start(bf16[128,1152]{1,0:T(8,128)(2,1)S(1)} %collective-permute-done), channel_id=1, source_target_pairs={{0,2},{2,4},{4,6},{1,3},{3,5},{5,7},{8,10},{10,12},{12,14},{9,11},... | collective-permute-start | bytes 884744 | tf_op jit(solution)/shard_map/ppermute | solution.py:144
  150.5 11.1 %collective-permute-start.3 = (bf16[128,1152]{1,0:T(8,128)(2,1)S(1)}, bf16[128,1152]{1,0:T(8,128)(2,1)S(1)}, u32[]{:S(2)}, u32[]{:S(2)}) collective-permute-start(bf16[128,1152]{1,0:T(8,128)(2,1)S(1)} %collective-permute-done.2), channel_id=1, source_target_pairs={{2,0},{4,2},{6,4},{3,1},{5,3},{7,5},{10,8},{12,10},{14,12},{11,9},... | collective-permute-start | bytes 884744 | tf_op jit(solution)/shard_map/ppermute | solution.py:145
  151.8 10.9 %collective-permute-start.5 = (bf16[128,1152]{1,0:T(8,128)(2,1)S(1)}, bf16[128,1152]{1,0:T(8,128)(2,1)S(1)}, u32[]{:S(2)}, u32[]{:S(2)}) collective-permute-start(bf16[128,1152]{1,0:T(8,128)(2,1)S(1)} %collective-permute-done.4), channel_id=1, source_target_pairs={{0,2},{2,4},{4,6},{1,3},{3,5},{5,7},{8,10},{10,12},{12,14},{9,11},... | collective-permute-start | bytes 884744 | tf_op jit(solution)/shard_map/ppermute | solution.py:144
  164.5 1.2 copy-start.8
  179.7 7.7 %copy-start.20 = (s32[4]{0:T(128)S(1)}, s32[4]{0:T(128)}, u32[]{:S(2)}) copy-start(s32[4]{0:T(128)} %param.18) | copy-start | bytes 52
  179.7 9.0 %copy-start.17 = (f32[3,1152]{1,0:T(4,128)S(1)}, f32[3,1152]{1,0:T(4,128)}, u32[]{:S(2)}) copy-start(f32[3,1152]{1,0:T(4,128)} %param.28) | copy-start | bytes 41476
  181.8 14.6 %all-to-all-start = ((bf16[4,128,288]{1,2,0:T(8,128)(2,1)}), bf16[4,128,288]{1,2,0:T(8,128)(2,1)S(1)}, u32[]{:S(2)}, u32[]{:S(2)}) async-start(bf16[4,128,288]{1,2,0:T(8,128)(2,1)} %gather_fusion.2), calls=%async_computation | async-start | bytes 589824 | tf_op jit(solution)/shard_map/all_to_all | solution.py:161
  196.6 2.3 copy-start.6
  201.6 13.3 %all-to-all-start.1 = ((bf16[1,2,64,1152]{3,1,0,2:T(2,128)(2,1)}), bf16[1,2,64,1152]{3,1,0,2:T(2,128)(2,1)S(1)}, u32[]{:S(2)}, u32[]{:S(2)}) async-start(bf16[1,2,64,1152]{3,1,0,2:T(2,128)(2,1)} %copy.96), calls=%async_computation.1 | async-start | bytes 589824 | tf_op jit(solution)/shard_map/all_to_all | solution.py:166
  217.0 4.0 %copy-start.2 = (bf16[1,1152,4608]{2,1,0:T(8,128)(2,1)S(1)}, bf16[1,1152,4608]{2,1,0:T(8,128)(2,1)}, u32[]{:S(2)}) copy-start(bf16[1,1152,4608]{2,1,0:T(8,128)(2,1)} %all-gather.15.cloned.1.call-done) | copy-start | bytes 31850500
  231.5 4.0 %copy-start.3 = (bf16[1,1152,4608]{2,1,0:T(8,128)(2,1)S(1)}, bf16[1,1152,4608]{2,1,0:T(8,128)(2,1)}, u32[]{:S(2)}) copy-start(bf16[1,1152,4608]{2,1,0:T(8,128)(2,1)} %all-gather.15.cloned.1.call-done) | copy-start | bytes 31850500
  235.5 2.1 copy-start.1
  (1 other events, 0.7 us)
Sparse Core Ops, SparseCore 0:
  9.3 55.2 all-gather.8
  66.5 41.3 all-gather.10
  109.8 38.9 all-gather.12
  150.5 66.5 all-gather.14
